TPU v7x, 512 devices: a whole 4x4x16 slice. The times are simulated.
512 devices in a mesh: tm: 32 (over z, core), dp: 8 (over x_lo, y), rep: 2 (over x_hi).
Axes of the slice: x: 4 (x_hi: 2, x_lo: 2; x = x_hi * 2 + x_lo), y: 4, z: 16, core: 2. Of those that a mesh axis runs over, the one named last changes fastest.
Arguments:
- clip_frames: bfloat16 [16, 128, 32, 4, 256], P(('dp', 'rep'), 'tm'), may hold values from -6 to 6
- conv_weight: bfloat16 [3, 3, 3, 256, 256], replicated, may hold values from -0.078125 to 0.078125
- up_weight: bfloat16 [256, 1024], replicated, may hold values from -0.375 to 0.375
- cotangent: bfloat16 [16, 128, 32, 4, 1024], P(('dp', 'rep'), None, 'tm'), may hold values from -6 to 6
Outputs:
- input_grad: bfloat16 [16, 128, 32, 4, 256], P(('dp', 'rep'), 'tm')
- up_grad: float32 [256, 1024], P('tm', ('dp', 'rep'))
All inputs are finite; a program needn't handle non-finite values.
Results may differ from a plain program's by a relative error of at most 0.012.
Values may be sent and summed in bfloat16 or wider, within the bound.
A program may use at most 128 MiB of HBM per device.

v0:
```python
import math

import jax
import jax.numpy as jnp
from jax import lax
from jax.sharding import PartitionSpec as P


def from_behind(value, axis, steps):
    count = lax.axis_size(axis)
    initial, last = (max(0, -steps), min(count, count - steps))
    return lax.ppermute(value, axis, [(source, source + steps) for source in range(initial, last)])


def correlate(source, kernel, frames):
    rows = source.shape[1] - 2
    cols = source.shape[2] - 2
    patches = []
    for shift_t in range(3):
        for shift_r in range(3):
            for shift_c in range(3):
                patches.append(
                    source[
                        shift_t : shift_t + frames,
                        shift_r : shift_r + rows,
                        shift_c : shift_c + cols,
                    ]
                )
    stacked = jnp.concatenate(patches, axis=-1)
    width = stacked.shape[-1]
    flat_kernel = kernel.reshape(width, kernel.shape[-1])
    return jnp.dot(stacked.reshape(-1, width), flat_kernel, preferred_element_type=jnp.float32)


def pad_space(field):
    return jnp.pad(field, ((0, 0), (1, 1), (1, 1), (0, 0)))


def local(clip_frames, conv_weight, up_weight, cotangent):
    frames_local = clip_frames[0]
    frames = frames_local.shape[0]
    rows = frames_local.shape[1]
    cols = frames_local.shape[2]
    chans = frames_local.shape[3]
    is_first = lax.axis_index("tm") == 0
    earlier = from_behind(frames_local[frames - 2 :], "tm", 1)
    earlier = jnp.where(is_first, jnp.broadcast_to(frames_local[:1], earlier.shape), earlier)
    source = pad_space(jnp.concatenate([earlier, frames_local], axis=0))
    pre = correlate(source, conv_weight, frames)
    hidden = jax.nn.silu(pre).astype(jnp.bfloat16).reshape(1, frames, rows, cols, chans)
    contract_rows = (((0,), (0,)), ((), ()))
    contract_cols = (((1,), (1,)), ((), ()))
    row_hidden = lax.all_to_all(hidden, "tm", split_axis=2, concat_axis=1, tiled=True)
    flat_h = row_hidden.reshape(-1, chans)
    flat_g = cotangent.reshape(-1, cotangent.shape[-1])
    term = lax.dot_general(flat_h, flat_g, contract_rows, preferred_element_type=jnp.float32)
    row_grad = lax.dot_general(
        flat_g, up_weight, contract_cols, preferred_element_type=jnp.float32
    ).astype(jnp.bfloat16)
    hidden_grad = lax.all_to_all(
        row_grad.reshape(row_hidden.shape), "tm", split_axis=1, concat_axis=2, tiled=True
    )
    sigma = jax.nn.sigmoid(pre)
    slope = sigma * (1.0 + pre * (1.0 - sigma))
    pre_grad = (hidden_grad.reshape(-1, chans).astype(jnp.float32) * slope).astype(jnp.bfloat16)
    pre_grad = pre_grad.reshape(frames, rows, cols, chans)
    later = from_behind(pre_grad[:2], "tm", -1)
    back_kernel = jnp.transpose(conv_weight[::-1, ::-1, ::-1], (0, 1, 2, 4, 3))
    grad_source = pad_space(jnp.concatenate([pre_grad, later], axis=0))
    input_grad = correlate(grad_source, back_kernel, frames).reshape(frames, rows, cols, chans)

    def edge_term():
        start = jnp.concatenate(
            [jnp.zeros((2, rows, cols, chans), jnp.bfloat16), pre_grad[:2]], axis=0
        )
        parts = correlate(pad_space(start), back_kernel, 2).reshape(2, rows, cols, chans)
        return parts[0] + parts[1]

    def no_term():
        return jnp.zeros((rows, cols, chans), jnp.float32)

    edge = lax.cond(is_first, edge_term, no_term)
    input_grad = input_grad.at[0].add(edge)
    time_count = lax.axis_size("tm")
    clip_count = lax.axis_size(("dp", "rep"))
    factor = 1.0 / math.sqrt(clip_count * frames * time_count * rows * cols)
    part = lax.psum_scatter(term, "tm", scatter_dimension=0, tiled=True)
    summed = lax.psum_scatter(part, ("dp", "rep"), scatter_dimension=1, tiled=True)
    return (input_grad.astype(jnp.bfloat16)[None], summed * factor)


def solution(mesh):
    in_specs = (
        P(("dp", "rep"), "tm", None, None, None),
        P(),
        P(),
        P(("dp", "rep"), None, "tm", None, None),
    )
    out_specs = (P(("dp", "rep"), "tm", None, None, None), P("tm", ("dp", "rep")))
    return jax.shard_map(local, mesh=mesh, in_specs=in_specs, out_specs=out_specs, check_vma=False)
```

profile of v0, /device:TPU:32, one launch (start us, length us, event | category | flops | bytes accessed | tf_op | source)
XLA Modules:
  0.0 382.3 jit_solution(11873751514262837852)
XLA Ops:
  8.2 1.9 collective-permute-start
  10.1 1.3 reshape.131
  12.7 16.1 %all-to-all-start = ((bf16[1,128,1,4,256]{4,3,2,0,1:T(4,128)(2,1)}), bf16[1,128,1,4,256]{4,3,2,0,1:T(4,128)(2,1)S(1)}, u32[]{:S(2)}, u32[]{:S(2)}) async-start(bf16[1,128,1,4,256]{4,3,2,0,1:T(4,128)(2,1)} %bitcast.1), calls=%async_computation | async-start | bytes 524288 | tf_op jit(solution)/shard_map/all_to_all | solution.py:60
  30.7 6.0 %copy.26 = bf16[3,3,3,256,256]{3,4,2,1,0:T(8,128)(2,1)} copy(bf16[3,3,3,256,256]{4,3,2,1,0:T(8,128)(2,1)} %param.9) | data formatting | bytes 7077888 | tf_op args[1]
  36.7 4.3 %rev.3 = bf16[3,3,3,256,256]{3,4,2,1,0:T(8,128)(2,1)} reverse(bf16[3,3,3,256,256]{3,4,2,1,0:T(8,128)(2,1)} %copy.26), dimensions={0,1,2} | reverse | bytes 7077888 | tf_op jit(solution)/shard_map/rev | solution.py:68
  41.0 4.2 %reverse_bitcast_fusion = bf16[3,3,3,256,256]{4,3,2,1,0:T(8,128)(2,1)} fusion(bf16[3,3,3,256,256]{3,4,2,1,0:T(8,128)(2,1)} %copy.26), kind=kLoop, calls=%fused_computation.175 | loop fusion | bytes 7077888 | tf_op jit(solution)/shard_map/transpose | solution.py:68
  45.5 4.1 %pad_slice_fusion.24 = (bf16[4,32,4,256]{3,2,1,0:T(4,128)(2,1)}, bf16[4,32,4,256]{3,2,1,0:T(4,128)(2,1)}, bf16[4,32,4,256]{3,2,1,0:T(4,128)(2,1)}, bf16[4,32,4,2...) fusion(bf16[6,32,4,256]{3,2,1,0:T(4,128)(2,1)S(1)} %pad_maximum, ...), kind=kLoop, calls=%fused_computation.52 | loop fusion | bytes 5373952 | tf_op jit(solution)/shard_map/slice | solution.py:23
  49.7 1.5 pad_slice_fusion.25
  51.5 1.7 concatenate.77
  54.0 1.8 concatenate.78
  55.8 1.7 concatenate.79
  58.3 1.7 concatenate.81
  60.0 1.7 concatenate.82
  61.7 1.7 concatenate.83
  63.4 1.7 concatenate.84
  65.1 1.7 concatenate.85
  66.9 1.7 concatenate.86
  68.6 1.7 concatenate.87
  70.3 1.7 concatenate.88
  72.8 1.7 concatenate.90
  74.5 1.7 concatenate.91
  76.2 1.7 concatenate.92
  77.9 1.7 concatenate.93
  79.6 1.7 concatenate.94
  81.3 1.7 concatenate.95
  86.1 1.8 constant_dynamic-update-slice_fusion.26
  87.9 1.7 constant_dynamic-update-slice_fusion.25
  89.7 1.7 constant_dynamic-update-slice_fusion.24
  91.4 1.7 constant_dynamic-update-slice_fusion.23
  93.1 1.7 constant_dynamic-update-slice_fusion.22
  94.7 1.7 constant_dynamic-update-slice_fusion.21
  96.4 1.7 constant_dynamic-update-slice_fusion.20
  98.1 1.7 constant_dynamic-update-slice_fusion.19
  99.8 1.7 constant_dynamic-update-slice_fusion.18
  101.5 1.7 constant_dynamic-update-slice_fusion.17
  103.2 1.7 constant_dynamic-update-slice_fusion.16
  104.9 1.7 constant_dynamic-update-slice_fusion.15
  106.6 1.7 constant_dynamic-update-slice_fusion.14
  108.3 1.7 constant_dynamic-update-slice_fusion.13
  119.5 6.1 %multiply_convert_fusion = (bf16[512,256]{1,0:T(8,128)(2,1)S(1)}, bf16[512,256]{1,0:T(8,128)(2,1)S(1)}) fusion(f32[512,256]{1,0:T(8,128)S(1)} %reshape.138, bf16[512,6912]{1,0:T(8,128)(2,1)} %constant_dynamic-update-slice_fusion.1, bf16[6912,256]{1,0:T(8,128)(2,1)} %bitcast.46), kind=kOutput, calls=%fused_computation.102 | convolution fusion | flops 1813381120 | bytes 11665408 | tf_op jit(solution)/shard_map/dot_general | solution.py:32
  125.7 2.0 collective-permute-start.1
  128.6 12.4 %all-to-all-start.1 = ((bf16[1,4,32,4,256]{4,3,1,0,2:T(4,128)(2,1)}), bf16[1,4,32,4,256]{4,3,1,0,2:T(4,128)(2,1)S(1)}, u32[]{:S(2)}, u32[]{:S(2)}) async-start(bf16[1,4,32,4,256]{4,3,1,0,2:T(4,128)(2,1)} %copy.28), calls=%async_computation.1 | async-start | bytes 524288 | tf_op jit(solution)/shard_map/all_to_all | solution.py:53
  156.2 5.8 %all-to-all-done.1 = bf16[1,4,32,4,256]{4,3,1,0,2:T(4,128)(2,1)S(1)} async-done(((bf16[1,4,32,4,256]{4,3,1,0,2:T(4,128)(2,1)}), bf16[1,4,32,4,256]{4,3,1,0,2:T(4,128)(2,1)S(1)}, u32[]{:S(2)}, u32[]{:S(2)}) %all-to-all-start.1) | async-done | bytes 262176 | tf_op jit(solution)/shard_map/all_to_all | solution.py:53
  162.1 1.4 fusion.53
  170.0 6.0 %fusion.52 = f32[4,32,4,256]{3,1,2,0:T(8,128)S(1)} fusion(bf16[4,32,4,6912]{3,1,2,0:T(8,128)(2,1)} %fusion.49, bf16[6912,256,1,1]{1,0,3,2:T(8,128)(2,1)} %bitcast.47), kind=kOutput, calls=%fused_computation.177 | convolution fusion | flops 1811939328 | bytes 11141120 | tf_op jit(solution)/shard_map/dot_general | solution.py:32
  176.0 109.4 %reduce-scatter.5.cloned.1.call-done = f32[8,1024]{1,0:T(8,128)} async-done(((f32[256,1024]{1,0:T(8,128)}), f32[8,1024]{1,0:T(8,128)}) %reduce-scatter.5.cloned.1.call-update) | async-done | bytes 32784 | tf_op jit(solution)/shard_map/reduce_scatter | solution.py:87
  285.4 1.8 copy.31
  288.1 86.0 %reduce-scatter.7.cloned.1.call-done = f32[64,8]{1,0:T(8,128)} async-done(((f32[1024,8]{1,0:T(8,128)}), f32[64,8]{1,0:T(8,128)}) %reduce-scatter.7.cloned.1.call-update) | async-done | bytes 2064
  (104 shorter events, 44.6 us)
Async XLA Ops:
  7.2 4.3 %copy-start = (bf16[256,1024]{1,0:T(8,128)(2,1)S(1)}, bf16[256,1024]{1,0:T(8,128)(2,1)}, u32[]{:S(2)}) copy-start(bf16[256,1024]{1,0:T(8,128)(2,1)} %param.10) | copy-start | bytes 1572868
  8.2 37.1 %collective-permute-start = (bf16[2,32,4,256]{3,2,1,0:T(4,128)(2,1)S(1)}, bf16[2,32,4,256]{3,2,1,0:T(4,128)(2,1)S(1)}, u32[]{:S(2)}, u32[]{:S(2)}) collective-permute-start(bf16[2,32,4,256]{3,2,1,0:T(4,128)(2,1)S(1)} %slice_bitcast_fusion), channel_id=1, source_target_pairs={{0,16},{16,32},{32,48},{48,64},{64,80},{80,96},{96,112},{112,128},... | collective-permute-start | bytes 393224 | tf_op jit(solution)/shard_map/ppermute | solution.py:12
  12.7 106.5 %all-to-all-start = ((bf16[1,128,1,4,256]{4,3,2,0,1:T(4,128)(2,1)}), bf16[1,128,1,4,256]{4,3,2,0,1:T(4,128)(2,1)S(1)}, u32[]{:S(2)}, u32[]{:S(2)}) async-start(bf16[1,128,1,4,256]{4,3,2,0,1:T(4,128)(2,1)} %bitcast.1), calls=%async_computation | async-start | bytes 524288 | tf_op jit(solution)/shard_map/all_to_all | solution.py:60
  36.7 8.6 %copy-start.1 = (bf16[1,4,32,4,256]{4,3,2,1,0:T(4,128)(2,1)S(1)}, bf16[1,4,32,4,256]{4,3,2,1,0:T(4,128)(2,1)}, u32[]{:S(2)}) copy-start(bf16[1,4,32,4,256]{4,3,2,1,0:T(4,128)(2,1)} %param.8) | copy-start | bytes 786436
  53.3 29.8 %copy-start.10 = (bf16[4,32,4,256]{3,2,1,0:T(4,128)(2,1)S(1)}, bf16[4,32,4,256]{3,2,1,0:T(4,128)(2,1)}, u32[]{:S(2)}) copy-start(bf16[4,32,4,256]{3,2,1,0:T(4,128)(2,1)} %get-tuple-element.51) | copy-start | bytes 786436
  54.0 29.9 %copy-start.8 = (bf16[4,32,4,256]{3,2,1,0:T(4,128)(2,1)S(1)}, bf16[4,32,4,256]{3,2,1,0:T(4,128)(2,1)}, u32[]{:S(2)}) copy-start(bf16[4,32,4,256]{3,2,1,0:T(4,128)(2,1)} %get-tuple-element.55) | copy-start | bytes 786436
  58.3 25.6 %copy-start.9 = (bf16[4,32,4,256]{3,2,1,0:T(4,128)(2,1)S(1)}, bf16[4,32,4,256]{3,2,1,0:T(4,128)(2,1)}, u32[]{:S(2)}) copy-start(bf16[4,32,4,256]{3,2,1,0:T(4,128)(2,1)} %get-tuple-element.54) | copy-start | bytes 786436
  86.1 23.9 %copy-start.7 = (bf16[512,256]{1,0:T(8,128)(2,1)S(1)}, bf16[512,256]{1,0:T(8,128)(2,1)}, u32[]{:S(2)}) copy-start(bf16[512,256]{1,0:T(8,128)(2,1)} %concatenate.91) | copy-start | bytes 786436
  86.1 24.7 %copy-start.6 = (bf16[512,256]{1,0:T(8,128)(2,1)S(1)}, bf16[512,256]{1,0:T(8,128)(2,1)}, u32[]{:S(2)}) copy-start(bf16[512,256]{1,0:T(8,128)(2,1)} %concatenate.92) | copy-start | bytes 786436
  86.1 25.4 %copy-start.5 = (bf16[512,256]{1,0:T(8,128)(2,1)S(1)}, bf16[512,256]{1,0:T(8,128)(2,1)}, u32[]{:S(2)}) copy-start(bf16[512,256]{1,0:T(8,128)(2,1)} %concatenate.93) | copy-start | bytes 786436
  86.1 26.2 %copy-start.4 = (bf16[512,256]{1,0:T(8,128)(2,1)S(1)}, bf16[512,256]{1,0:T(8,128)(2,1)}, u32[]{:S(2)}) copy-start(bf16[512,256]{1,0:T(8,128)(2,1)} %concatenate.94) | copy-start | bytes 786436
  86.1 26.9 %copy-start.3 = (bf16[512,256]{1,0:T(8,128)(2,1)S(1)}, bf16[512,256]{1,0:T(8,128)(2,1)}, u32[]{:S(2)}) copy-start(bf16[512,256]{1,0:T(8,128)(2,1)} %concatenate.95) | copy-start | bytes 786436
  86.1 27.7 %copy-start.2 = (bf16[512,256]{1,0:T(8,128)(2,1)S(1)}, bf16[512,256]{1,0:T(8,128)(2,1)}, u32[]{:S(2)}) copy-start(bf16[512,256]{1,0:T(8,128)(2,1)} %concatenate.96) | copy-start | bytes 786436
  125.7 15.6 %collective-permute-start.1 = (bf16[2,32,4,256]{3,1,2,0:T(8,128)(2,1)S(1)}, bf16[2,32,4,256]{3,1,2,0:T(8,128)(2,1)S(1)}, u32[]{:S(2)}, u32[]{:S(2)}) collective-permute-start(bf16[2,32,4,256]{3,1,2,0:T(8,128)(2,1)S(1)} %copy.23), channel_id=1, source_target_pairs={{16,0},{32,16},{48,32},{64,48},{80,64},{96,80},{112,96},{128,112},... | collective-permute-start | bytes 393224 | tf_op jit(solution)/shard_map/ppermute | solution.py:12
  128.6 33.4 %all-to-all-start.1 = ((bf16[1,4,32,4,256]{4,3,1,0,2:T(4,128)(2,1)}), bf16[1,4,32,4,256]{4,3,1,0,2:T(4,128)(2,1)S(1)}, u32[]{:S(2)}, u32[]{:S(2)}) async-start(bf16[1,4,32,4,256]{4,3,1,0,2:T(4,128)(2,1)} %copy.28), calls=%async_computation.1 | async-start | bytes 524288 | tf_op jit(solution)/shard_map/all_to_all | solution.py:53
  141.0 144.3 %reduce-scatter.5.cloned.1.call-start = ((), (), s32[]{:S(2)}) async-start(), calls=%async_computation.4 | async-start | bytes 1081344 | tf_op jit(solution)/shard_map/reduce_scatter | solution.py:87
  163.5 210.5 %reduce-scatter.7.cloned.1.call-start = ((), (), s32[]{:S(2)}) async-start(), calls=%async_computation.5 | async-start | bytes 557056
Sparse Core Ops, SparseCore 0:
  163.7 121.6 reduce-scatter.4
  288.4 85.6 reduce-scatter.6
where the time goes:
time: 384 us; the launch traced here: 382 us
  waiting for transfers between devices  201 us (52%)
  local copies, waits for them, and re-layouts  119 us (31%)
  starting transfers between devices  32.5 us (8%)
  between operations  14.4 us (4%)
  matrix products  14 us (4%)
    reduce_scatter x1, waiting for transfers between devices, local(): part = lax.psum_scatter(term, 'tm', scatter_dimension=0, tiled=True)  109 us
    unnamed x3, waiting for transfers between devices  86 us
    unnamed x79, local copies, waits for them, and re-layouts  63 us
    concatenate x29, local copies, waits for them, and re-layouts, correlate(): stacked = jnp.concatenate(patches, axis=-1)  36.3 us
    all_to_all x1, starting transfers between devices, local(): lax.all_to_all(row_grad.reshape(row_hidden.shape), 'tm', split_axis=1, co...  16.1 us
    all_to_all x1, starting transfers between devices, local(): lax.all_to_all(hidden, 'tm', split_axis=2, concat_axis=1, tiled=True)  12.4 us
    dot_general x2, matrix products, correlate(): jnp.dot(stacked.reshape(-1, width), flat_kernel, preferred_element_type=j...  12.1 us
  transfers between devices with their start and end apart: 6, of which 3 were waited for; matrix products, arithmetic and copies ran while one was open for 32% of the time, Pallas kernels for 0%

commit v1 on v0

v1 whole, which is shorter than its diff:
```python
import functools
import math

import jax
import jax.numpy as jnp
from jax import lax
from jax.experimental import pallas as pl
from jax.experimental.pallas import tpu as pltpu
from jax.sharding import PartitionSpec as P

MESH = pl.DeviceIdType.MESH
BF16 = jnp.bfloat16
F32 = jnp.float32
LANES = (slice(0, 128), slice(128, 256))


def dot_nn(a, b):
    return lax.dot_general(a, b, (((1,), (0,)), ((), ())), preferred_element_type=F32)


def dot_nt(a, b):
    return lax.dot_general(a, b, (((1,), (1,)), ((), ())), preferred_element_type=F32)


def kernel(n, J, R, factor, x_ref, w_hbm, u_ref, g_ref, out_ref, ug_ref,
           w, wt, gt, rg, hg, hid, hidr, hf, ph, phr, x32, p32, q32, s, pre, slope, of32,
           r1s, r1r, keep, r2s, r2r, r3s, r3r,
           w_sem, hf_sem, ph_sem, hg_sem, hid_sem, r1_sem, r2_sem, r3_send, r3_recv):
    H = n
    C = 256
    FW = 16
    HALF = 2 * 4 * H
    XP = 4 * H + 16
    QP = H + 16
    CB = 1024 // J
    RB = C // n
    me = lax.axis_index("tm")
    dp = lax.axis_index("dp")
    rep = lax.axis_index("rep")
    core = lax.rem(me, 2)
    myj = dp * R + rep
    is_first = me == 0
    is_last = me == n - 1

    def offset(k):
        return lax.rem(jnp.where(lax.rem(k, 2) == 1, (k + 1) // 2, n - k // 2), n)

    def peer(k):
        return lax.rem(me + offset(k), n)

    def block(i):
        return pl.ds(pl.multiple_of(i * FW, FW), FW)

    def to_tm(src, dst, sems, target):
        return pltpu.make_async_remote_copy(
            src_ref=src, dst_ref=dst, send_sem=sems.at[0], recv_sem=sems.at[1],
            device_id=(target, dp, rep), device_id_type=MESH)

    def to_xy(src, dst, sems, j):
        return pltpu.make_async_remote_copy(
            src_ref=src, dst_ref=dst, send_sem=sems.at[0], recv_sem=sems.at[1],
            device_id=(me, j // R, lax.rem(j, R)), device_id_type=MESH)

    barrier = pltpu.get_barrier_semaphore()
    wcopy = pltpu.make_async_copy(w_hbm, w, w_sem)
    wcopy.start()

    def greet_tm(k, _):
        pl.semaphore_signal(barrier, inc=1, device_id=(lax.rem(me + k, n), dp, rep), device_id_type=MESH)
        return 0

    def greet_xy(k, _):
        j = lax.rem(myj + k, J)
        pl.semaphore_signal(barrier, inc=1, device_id=(me, j // R, lax.rem(j, R)), device_id_type=MESH)
        return 0

    lax.fori_loop(1, n, greet_tm, 0)
    lax.fori_loop(1, J, greet_xy, 0)

    rg[...] = dot_nt(g_ref[...], u_ref[...]).astype(BF16)
    hg[block(me), :] = rg[block(me), :]

    pl.semaphore_wait(barrier, n - 1 + J - 1)

    halo = to_tm(x_ref.at[pl.ds(HALF, HALF)], hf, hf_sem, lax.rem(me + 1, n))

    @pl.when(jnp.logical_not(is_last))
    def _():
        halo.start()

    def send_hg(k, _):
        to = peer(k)
        to_tm(rg.at[block(to)], hg.at[block(me)], hg_sem, to).start()
        return 0

    lax.fori_loop(1, n, send_hg, 0)

    for f in range(6):
        x32[:, pl.ds(f * XP, 8), :] = jnp.zeros((2, 8, 128), F32)
        x32[:, pl.ds(f * XP + 8 + 4 * H, 8), :] = jnp.zeros((2, 8, 128), F32)
    for f in range(6):
        s[f, 0:H, :] = jnp.zeros((H, 3 * C), BF16)
        s[f, 5 * H : 6 * H, :] = jnp.zeros((H, 3 * C), BF16)

    def put_frame(f, ref, source):
        for e in range(2):
            x32[e, pl.ds(f * XP + 8, 4 * H), :] = ref[pl.ds(source * 4 * H, 4 * H), LANES[e]].astype(F32)

    for f in range(2, 6):
        put_frame(f, x_ref, f - 2)

    def shifts(f, _):
        for col in range(4):
            for b in range(3):
                for e in range(2):
                    v = x32[e, pl.ds(f * XP + 8 + (b - 1) * 4 + col, H, stride=4), :]
                    s[f, (col + 1) * H : (col + 2) * H, b * C + e * 128 : b * C + (e + 1) * 128] = v.astype(BF16)
        return 0

    lax.fori_loop(2, 6, shifts, 0)
    wcopy.wait()

    def set_pre(value):
        for e in range(2):
            pre[e] = value[:, LANES[e]]

    def add_pre(value):
        for e in range(2):
            pre[e] += value[:, LANES[e]]

    def conv_step(a, c):
        lhs = s[pl.ds(a, 4), pl.ds(pl.multiple_of(c * H, H), 4 * H), :].reshape(16 * H, 3 * C)
        return dot_nn(lhs, w[a, :, c].reshape(3 * C, C))

    set_pre(conv_step(2, 0))

    def conv_fwd(k, _):
        add_pre(conv_step(2 - k // 3, lax.rem(k, 3)))
        return 0

    lax.fori_loop(1, 3, conv_fwd, 0)

    @pl.when(jnp.logical_not(is_last))
    def _():
        halo.wait_send()

    @pl.when(jnp.logical_not(is_first))
    def _():
        halo.wait_recv()
        for f in range(2):
            put_frame(f, hf, f)

    @pl.when(is_first)
    def _():
        for f in range(2):
            put_frame(f, x_ref, 0)

    lax.fori_loop(0, 2, shifts, 0)
    lax.fori_loop(3, 9, conv_fwd, 0)

    def act(group, _):
        for u in range(4):
            k = group * 4 + u
            to = peer(k)
            for e in range(2):
                v = pre[e, pl.ds(to, FW, stride=H), :]
                sig = 1.0 / (1.0 + jnp.exp(-v))
                hid[block(to), LANES[e]] = (v * sig).astype(BF16)
                slope[block(to), LANES[e]] = sig * (1.0 + v * (1.0 - sig))
        for u in range(4):
            k = group * 4 + u
            to = peer(k)

            @pl.when(k > 0)
            def _():
                to_tm(hid.at[block(to)], hidr.at[block(me)], hid_sem, to).start()
        return 0

    lax.fori_loop(0, n // 4, act, 0)
    hidr[block(me), :] = hid[block(me), :]

    def flip_g(i, _):
        at = pl.multiple_of(i * 128, 128)
        gt[pl.ds(at, 128), :] = g_ref[:, pl.ds(at, 128)].T
        return 0

    lax.fori_loop(0, 8, flip_g, 0)

    def flip_w(k, _):
        a, c = k // 3, lax.rem(k, 3)
        for b in range(3):
            wt[k, b * C : (b + 1) * C, :] = w[2 - a, 2 - b, 2 - c].T
        return 0

    lax.fori_loop(0, 9, flip_w, 0)

    def all_blocks(src, dst, sems):
        most = pl.ds(0, (n - 1) * FW)
        return to_tm(src.at[most], dst.at[most], sems, lax.rem(me + 1, n))

    done_hid = all_blocks(hid, hidr, hid_sem)
    done_hid.wait_recv()
    theirs = pl.ds(pl.multiple_of((1 - core) * 128, 128), 128)
    mine = pl.ds(pl.multiple_of(core * 128, 128), 128)
    r1s[...] = dot_nn(gt[...], hidr[:, theirs]).astype(BF16)
    pair = to_tm(r1s, r1r, r1_sem, me + 1 - 2 * core)
    pair.start()
    keep[...] = dot_nn(gt[...], hidr[:, mine])
    pair.wait()
    keep[...] += r1r[...].astype(F32)
    r2s[...] = keep[...].astype(BF16)

    def rows_of(j):
        return pl.ds(pl.multiple_of(j * CB, CB), CB)

    def send_r2(k, _):
        j = lax.rem(myj + k, J)
        to_xy(r2s.at[rows_of(j)], r2r.at[rows_of(myj)], r2_sem, j).start()
        return 0

    lax.fori_loop(1, J, send_r2, 0)

    p32[:, pl.ds(0, FW), :] = jnp.zeros((2, FW, 128), F32)
    p32[:, pl.ds((H + 1) * FW, FW), :] = jnp.zeros((2, FW, 128), F32)
    done_hg = all_blocks(rg, hg, hg_sem)
    done_hg.wait_recv()
    grad = (hg[...].astype(F32) * slope[...]).astype(BF16)
    for e in range(2):
        p32[e, pl.ds(FW, H * FW), :] = grad[:, LANES[e]].astype(F32)

    def grad_shifts(t, _):
        for col in range(4):
            for b in range(3):
                for e in range(2):
                    v = p32[e, pl.ds(b * FW + t * 4 + col, H, stride=FW), :].astype(BF16)
                    s[t, (col + 1) * H : (col + 2) * H, b * C + e * 128 : b * C + (e + 1) * 128] = v
        return 0

    lax.fori_loop(0, 2, grad_shifts, 0)
    for t in range(2):
        ph[pl.ds(t * 4 * H, 4 * H), :] = s[t, H : 5 * H, C : 2 * C]
    back = to_tm(ph, phr, ph_sem, lax.rem(me + n - 1, n))

    @pl.when(jnp.logical_not(is_first))
    def _():
        back.start()

    lax.fori_loop(2, 4, grad_shifts, 0)

    @pl.when(is_first)
    def _():
        two = s[0].astype(F32) + s[1].astype(F32)
        s[6] = two.astype(BF16)
        s[7] = (two + s[2].astype(F32)).astype(BF16)

    def back_step(k):
        a, c = k // 3, lax.rem(k, 3)
        at = pl.ds(pl.multiple_of(c * H, H), 4 * H)
        head = jnp.where(jnp.logical_and(is_first, a > 0), a + 5, a)
        lhs = jnp.concatenate([s[pl.ds(head, 1), at, :], s[pl.ds(a + 1, 3), at, :]], axis=0)
        return dot_nn(lhs.reshape(16 * H, 3 * C), wt[k])

    set_pre(back_step(0))

    def conv_back(k, _):
        add_pre(back_step(k))
        return 0

    lax.fori_loop(1, 3, conv_back, 0)

    most_xy = pl.ds(0, (J - 1) * CB)
    done_r2 = to_xy(r2s.at[most_xy], r2r.at[most_xy], r2_sem, lax.rem(myj + 1, J))
    done_r2.wait_recv()
    r2r[rows_of(myj), :] = jnp.zeros((CB, 128), BF16)
    total = keep[rows_of(myj), :]
    for j in range(J):
        total = total + r2r[pl.ds(j * CB, CB), :].astype(F32)
    flipped = total.T
    for m in range(n // 2):
        r3s[m] = flipped[m * RB : (m + 1) * RB, :]

    z = me // 2

    def r3_copy(m):
        return pltpu.make_async_remote_copy(
            src_ref=r3s.at[m], dst_ref=r3r.at[z], send_sem=r3_send.at[m], recv_sem=r3_recv.at[z],
            device_id=(core * (n // 2) + m, dp, rep), device_id_type=MESH)

    def send_r3(m, _):
        @pl.when(core * (n // 2) + m != me)
        def _():
            r3_copy(m).start()

        @pl.when(core * (n // 2) + m == me)
        def _():
            r3r[z] = r3s[m]
        return 0

    lax.fori_loop(0, n // 2, send_r3, 0)

    for tw in range(8):
        q32[pl.ds(tw * QP, 8), :] = jnp.zeros((8, C), F32)
        q32[pl.ds(tw * QP + 8 + H, 8), :] = jnp.zeros((8, C), F32)

    @pl.when(jnp.logical_not(is_first))
    def _():
        back.wait_send()

    @pl.when(jnp.logical_not(is_last))
    def _():
        back.wait_recv()
        for tw in range(8):
            q32[pl.ds(tw * QP + 8, H), :] = phr[pl.ds(tw * H, H), :].astype(F32)

    @pl.when(is_last)
    def _():
        for tw in range(8):
            q32[pl.ds(tw * QP + 8, H), :] = jnp.zeros((H, C), F32)

    for t in range(2):
        for col in range(4):
            for b in range(3):
                v = q32[pl.ds((t * 4 + col) * QP + 7 + b, H), :].astype(BF16)
                s[4 + t, (col + 1) * H : (col + 2) * H, b * C : (b + 1) * C] = v

    lax.fori_loop(3, 9, conv_back, 0)

    for t in range(4):
        for col in range(4):
            for e in range(2):
                of32[e, pl.ds(t * 4 * H + col, H, stride=4), :] = pre[e, pl.ds((t * 4 + col) * H, H), :]
    for e in range(2):
        out_ref[:, LANES[e]] = of32[e].astype(BF16)

    def wait_r3(i, _):
        @pl.when(2 * i + me // (n // 2) != me)
        def _():
            pltpu.make_async_remote_copy(
                src_ref=r3s.at[i], dst_ref=r3r.at[i], send_sem=r3_send.at[i], recv_sem=r3_recv.at[i],
                device_id=(lax.rem(me + 1, n), dp, rep), device_id_type=MESH).wait_recv()

        @pl.when(core * (n // 2) + i != me)
        def _():
            r3_copy(i).wait_send()
        return 0

    lax.fori_loop(0, n // 2, wait_r3, 0)
    result = r3r[0]
    for i in range(1, n // 2):
        result = result + r3r[i]
    ug_ref[...] = result * factor

    done_hid.wait_send()
    done_hg.wait_send()
    done_r2.wait_send()


def local(n, J, R, clip_frames, conv_weight, up_weight, cotangent):
    C = conv_weight.shape[-1]
    H = n
    pixels = 16 * H
    factor = 1.0 / math.sqrt(J * 4 * n * H * 4)
    x = clip_frames.reshape(pixels, C)
    g = cotangent.reshape(16 * n, 4 * C)
    vmem = pl.BlockSpec(memory_space=pltpu.VMEM)
    pair = pltpu.SemaphoreType.DMA((2,))
    out, up = pl.pallas_call(
        functools.partial(kernel, n, J, R, factor),
        out_shape=(
            jax.ShapeDtypeStruct((pixels, C), BF16),
            jax.ShapeDtypeStruct((C // n, 4 * C // J), F32),
        ),
        in_specs=[vmem, pl.BlockSpec(memory_space=pl.ANY), vmem, vmem],
        out_specs=(vmem, vmem),
        scratch_shapes=[
            pltpu.VMEM((3, 3, 3, C, C), BF16),
            pltpu.VMEM((9, 3 * C, C), BF16),
            pltpu.VMEM((4 * C, 16 * n), BF16),
            pltpu.VMEM((16 * n, C), BF16),
            pltpu.VMEM((16 * n, C), BF16),
            pltpu.VMEM((16 * n, C), BF16),
            pltpu.VMEM((16 * n, C), BF16),
            pltpu.VMEM((8 * H, C), BF16),
            pltpu.VMEM((8 * H, C), BF16),
            pltpu.VMEM((8 * H, C), BF16),
            pltpu.VMEM((2, 6 * (4 * H + 16), 128), F32),
            pltpu.VMEM((2, (H + 2) * 16, 128), F32),
            pltpu.VMEM((8 * (H + 16), C), F32),
            pltpu.VMEM((8, 6 * H, 3 * C), BF16),
            pltpu.VMEM((2, pixels, 128), F32),
            pltpu.VMEM((pixels, C), F32),
            pltpu.VMEM((2, pixels, 128), F32),
            pltpu.VMEM((4 * C, C // 2), BF16),
            pltpu.VMEM((4 * C, C // 2), BF16),
            pltpu.VMEM((4 * C, C // 2), F32),
            pltpu.VMEM((4 * C, C // 2), BF16),
            pltpu.VMEM((4 * C, C // 2), BF16),
            pltpu.VMEM((n // 2, C // n, 4 * C // J), F32),
            pltpu.VMEM((n // 2, C // n, 4 * C // J), F32),
            pltpu.SemaphoreType.DMA,
            pair, pair, pair, pair, pair, pair,
            pltpu.SemaphoreType.DMA((n // 2,)),
            pltpu.SemaphoreType.DMA((n // 2,)),
        ],
        compiler_params=pltpu.CompilerParams(
            collective_id=0, has_side_effects=True, vmem_limit_bytes=48 * 1024 * 1024),
        cost_estimate=pl.CostEstimate(flops=4_200_000_000, bytes_accessed=6_000_000, transcendentals=131072),
    )(x, conv_weight, up_weight, g)
    return out.reshape(clip_frames.shape), up


def solution(mesh):
    in_specs = (
        P(("dp", "rep"), "tm", None, None, None),
        P(),
        P(),
        P(("dp", "rep"), None, "tm", None, None),
    )
    out_specs = (P(("dp", "rep"), "tm", None, None, None), P("tm", ("dp", "rep")))
    n = mesh.shape["tm"]
    R = mesh.shape["rep"]
    J = mesh.shape["dp"] * R
    return jax.shard_map(functools.partial(local, n, J, R), mesh=mesh, in_specs=in_specs,
                         out_specs=out_specs, check_vma=False)
```

time: 384 us -> 72.7 us (0.19)
  the two profiles are of different devices: /device:TPU:32 before, /device:TPU:1 now
where the time goes in v1:
time: 72.7 us; the launch traced here: 72.4 us
  Pallas kernels  65 us (89%)
  local copies, waits for them, and re-layouts  6.76 us (9%)
    pallas_call x1, Pallas kernels, local(): pl.pallas_call(functools.partial(kernel, n, J, R, factor), out_shape=(jax...  65 us
    unnamed x5, local copies, waits for them, and re-layouts  3.63 us

profile of v1, /device:TPU:1, one launch (start us, length us, event | category | flops | bytes accessed | tf_op | source)
XLA Modules:
  0.0 72.4 jit_solution(2461503132321978363)
XLA Ops:
  0.6 1.0 %reshape.13.x_ref = bf16[512,256]{1,0:T(8,128)(2,1)S(1)} reshape(bf16[1,4,32,4,256]{4,3,2,1,0:T(4,128)(2,1)} %param.4) | data formatting | bytes 524288 | tf_op jit(solution)/shard_map/reshape | solution.py:363
  1.6 1.3 %reshape.14.g_ref = bf16[512,1024]{1,0:T(8,128)(2,1)S(1)} reshape(bf16[1,128,1,4,1024]{4,3,2,1,0:T(4,128)(2,1)} %param.7) | data formatting | bytes 2097152 | tf_op jit(solution)/shard_map/reshape | solution.py:364
  3.0 0.0 copy-start
  3.0 2.0 %copy-done = bf16[3,3,3,256,256]{4,3,2,1,0:T(8,128)(2,1)S(1)} copy-done((bf16[3,3,3,256,256]{4,3,2,1,0:T(8,128)(2,1)S(1)}, bf16[3,3,3,256,256]{4,3,2,1,0:T(8,128)(2,1)}, u32[]{:S(2)}) %copy-start) | copy-done | bytes 3538968
  5.0 0.0 copy-start.1
  5.0 1.0 %copy-done.1 = bf16[256,1024]{1,0:T(8,128)(2,1)S(1)} copy-done((bf16[256,1024]{1,0:T(8,128)(2,1)S(1)}, bf16[256,1024]{1,0:T(8,128)(2,1)}, u32[]{:S(2)}) %copy-start.1) | copy-done | bytes 524312
  6.0 65.0 %shard_map.59 = (bf16[512,256]{1,0:T(8,128)(2,1)S(1)}, f32[8,64]{1,0:T(8,128)S(1)}) custom-call(bf16[512,256]{1,0:T(8,128)(2,1)S(1)} %reshape.13.x_ref, bf16[3,3,3,256,256]{4,3,2,1,0:T(8,128)(2,1)S(1)} %copy-done, bf16[256,1024]{1,0:T(8,128)(2,1)S(1)} %copy-done.1, bf16[512,1024]{1,0:T(8,128)(2,1)S(1)} %reshape.14.g_ref), custom_call_target="tpu_custom_call" | custom-call | flops 4200000000 | bytes 6000000 | tf_op jit(solution)/shard_map/pallas_call | solution.py:367
  71.1 0.8 %reshape.15 = bf16[1,4,32,4,256]{4,3,2,1,0:T(4,128)(2,1)} reshape(bf16[512,256]{1,0:T(8,128)(2,1)S(1)} %get-tuple-element.4) | data formatting | bytes 524288 | tf_op jit(solution)/shard_map/reshape | solution.py:409
  71.8 0.6 copy.7
Async XLA Ops:
  3.0 2.0 %copy-start = (bf16[3,3,3,256,256]{4,3,2,1,0:T(8,128)(2,1)S(1)}, bf16[3,3,3,256,256]{4,3,2,1,0:T(8,128)(2,1)}, u32[]{:S(2)}) copy-start(bf16[3,3,3,256,256]{4,3,2,1,0:T(8,128)(2,1)} %w_hbm.1) | copy-start | bytes 10616836
  5.0 1.0 %copy-start.1 = (bf16[256,1024]{1,0:T(8,128)(2,1)S(1)}, bf16[256,1024]{1,0:T(8,128)(2,1)}, u32[]{:S(2)}) copy-start(bf16[256,1024]{1,0:T(8,128)(2,1)} %u_ref.1) | copy-start | bytes 1572868

commit v2 on v1

v2 whole, which is shorter than its diff:
```python
import functools
import math

import jax
import jax.numpy as jnp
from jax import lax
from jax.experimental import pallas as pl
from jax.experimental.pallas import tpu as pltpu
from jax.sharding import PartitionSpec as P

MESH = pl.DeviceIdType.MESH
BF16 = jnp.bfloat16
F32 = jnp.float32
LANES = (slice(0, 128), slice(128, 256))


def dot_nn(a, b):
    return lax.dot_general(a, b, (((1,), (0,)), ((), ())), preferred_element_type=F32)


def dot_nt(a, b):
    return lax.dot_general(a, b, (((1,), (1,)), ((), ())), preferred_element_type=F32)


def kernel(n, J, R, factor, x_hbm, w_hbm, u_hbm, g_hbm, out_ref, ug_ref,
           xs, gs, g2, u, w, wt, gt, rg, hg, hid, hidr, hs, hf, ph, phr, x32, p32, q32, s, pre, slope, of32,
           r1s, r1r, keep, r2s, r2r, r3s, r3r,
           in_sem, hf_sem, ph_sem, hg_sem, hid_sem, r1_sem, r2_sem, r3_send, r3_recv):
    H = n
    C = 256
    FW = 16
    HALF = 8 * H
    XP = 4 * H + 16
    QP = H + 16
    CB = 4 * C // J
    WIDE = -(-CB // 128) * 128
    RB = C // n
    me = lax.axis_index("tm")
    dp = lax.axis_index("dp")
    rep = lax.axis_index("rep")
    core = lax.rem(me, 2)
    myj = dp * R + rep
    is_first = me == 0
    is_last = me == n - 1
    after = lax.rem(me + 1, n)
    before = lax.rem(me + n - 1, n)

    def peer(k):
        i = n - k
        return lax.rem(me + jnp.where(lax.rem(i, 2) == 1, (i + 1) // 2, n - i // 2), n)

    def block(i):
        return pl.ds(pl.multiple_of(i * FW, FW), FW)

    def to_tm(src, dst, sems, target):
        return pltpu.make_async_remote_copy(
            src_ref=src, dst_ref=dst, send_sem=sems.at[0], recv_sem=sems.at[1],
            device_id=(target, dp, rep), device_id_type=MESH)

    def to_xy(src, dst, sems, j):
        return pltpu.make_async_remote_copy(
            src_ref=src, dst_ref=dst, send_sem=sems.at[0], recv_sem=sems.at[1],
            device_id=(me, j // R, lax.rem(j, R)), device_id_type=MESH)

    barrier = pltpu.get_barrier_semaphore()
    quarters = [pl.ds(i * n, n) for i in range(4)]
    parts = [(x_hbm, xs)]
    parts += [(w_hbm.at[a, b], w.at[a, b]) for a in (2, 1, 0) for b in range(3)]
    parts += [(g_hbm.at[rows], gs.at[rows]) for rows in quarters] + [(u_hbm, u)]
    loads = [pltpu.make_async_copy(src, dst, in_sem.at[i]) for i, (src, dst) in enumerate(parts)]
    for load in loads:
        load.start()

    def greet_tm(k, _):
        pl.semaphore_signal(barrier, inc=1, device_id=(peer(k), dp, rep), device_id_type=MESH)
        return 0

    def greet_xy(k, _):
        j = lax.rem(myj + k, J)
        pl.semaphore_signal(barrier, inc=1, device_id=(me, j // R, lax.rem(j, R)), device_id_type=MESH)
        return 0

    lax.fori_loop(1, n, greet_tm, 0)
    lax.fori_loop(1, J, greet_xy, 0)

    for f in range(6):
        x32[:, pl.ds(f * XP, 8), :] = jnp.zeros((2, 8, 128), F32)
        x32[:, pl.ds(f * XP + 8 + 4 * H, 8), :] = jnp.zeros((2, 8, 128), F32)
    for f in range(6):
        s[f, 0:H, :] = jnp.zeros((H, 3 * C), BF16)
        s[f, 5 * H : 6 * H, :] = jnp.zeros((H, 3 * C), BF16)

    def put_frame(f, value):
        for e in range(2):
            x32[e, pl.ds(f * XP + 8, 4 * H), :] = value[:, LANES[e]]

    def own_frame(f):
        return xs[pl.ds(f * H, H)].astype(F32).reshape(4 * H, C)

    loads[0].wait()
    hs[...] = xs[pl.ds(2 * H, 2 * H)].reshape(HALF, C)

    for f in range(4):
        put_frame(f + 2, own_frame(f))

    def shifts(f, _):
        for col in range(4):
            for b in range(3):
                for e in range(2):
                    v = x32[e, pl.ds(f * XP + 8 + (b - 1) * 4 + col, H, stride=4), :]
                    s[f, (col + 1) * H : (col + 2) * H, b * C + e * 128 : b * C + (e + 1) * 128] = v.astype(BF16)
        return 0

    lax.fori_loop(2, 6, shifts, 0)
    def pieces(src, dst, sems, target):
        def one(i, _):
            to_tm(src.at[block(i)], dst.at[block(i)], sems, target).start()
            return 0
        lax.fori_loop(0, HALF // FW, one, 0)

    def open_up():
        pl.semaphore_wait(barrier, n - 1 + J - 1)

        @pl.when(jnp.logical_not(is_last))
        def _():
            pieces(hs, hf, hf_sem, after)


    pre[...] = jnp.zeros((2, 2 * HALF, 128), F32)
    for load in loads[1:10]:
        load.wait()

    def taps(first, second, pair, weights):
        value = None
        for c in range(3):
            at = pl.ds(c * H, 4 * H)
            lhs = jnp.concatenate([s[pl.ds(first, 1), at, :], s[pl.ds(second, 1), at, :]], axis=0)
            part = dot_nn(lhs.reshape(HALF, 3 * C), weights(c))
            value = part if value is None else value + part
        rows = pl.ds(pl.multiple_of(pair * HALF, HALF), HALF)
        for e in range(2):
            pre[e, rows, :] += value[:, LANES[e]]

    def conv_fwd(pair, a):
        first = a + 2 * pair
        taps(first, first + 1, pair, lambda c: w[a, :, c].reshape(3 * C, C))

    def conv_step(k, _):
        @pl.when(k == 4)
        def _():
            open_up()

            @pl.when(jnp.logical_not(is_first))
            def _():
                to_tm(hs, hf, hf_sem, after).wait_recv()
                for f in range(2):
                    put_frame(f, hf[pl.ds(f * 4 * H, 4 * H), :].astype(F32))

            @pl.when(is_first)
            def _():
                for f in range(2):
                    put_frame(f, own_frame(0))

            lax.fori_loop(0, 2, shifts, 0)

        conv_fwd(jnp.where(k < 3, 1, 0), jnp.where(k < 3, 2 - k, 5 - k))
        return 0

    lax.fori_loop(0, 6, conv_step, 0)

    def act(group, _):
        for i in range(4):
            to = peer(group * 4 + i + 1)
            for e in range(2):
                v = pre[e, pl.ds(to, FW, stride=H), :]
                sig = 0.5 + 0.5 * jnp.tanh(0.5 * v)
                hid[block(to), LANES[e]] = (v * sig).astype(BF16)
                slope[block(to), LANES[e]] = sig * (1.0 + v * (1.0 - sig))
        for i in range(4):
            k = group * 4 + i + 1
            to = peer(k)

            @pl.when(k < n)
            def _():
                to_tm(hid.at[block(to)], hidr.at[block(me)], hid_sem, to).start()
        return 0

    lax.fori_loop(0, n // 4, act, 0)
    for load in loads[10:14]:
        load.wait()

    def flatten_g(i, _):
        rows = pl.ds(pl.multiple_of(i * 64, 64), 64)
        g2[rows, :] = gs[pl.ds(i * 16, 16)].reshape(64, 4 * C)
        return 0

    lax.fori_loop(0, n // 4, flatten_g, 0)
    loads[14].wait()
    rg[...] = dot_nt(g2[...], u[...]).astype(BF16)
    hg[block(me), :] = rg[block(me), :]

    def send_hg(k, _):
        to = peer(k)
        to_tm(rg.at[block(to)], hg.at[block(me)], hg_sem, to).start()
        return 0

    lax.fori_loop(1, n, send_hg, 0)
    hidr[block(me), :] = hid[block(me), :]

    def flip_g(i, _):
        at = pl.multiple_of(i * 128, 128)
        gt[pl.ds(at, 128), :] = g2[:, pl.ds(at, 128)].T
        return 0

    lax.fori_loop(0, 8, flip_g, 0)

    def flip_w(k, _):
        a, c = k // 3, lax.rem(k, 3)
        for b in range(3):
            wt[k, b * C : (b + 1) * C, :] = w[2 - a, 2 - b, 2 - c].T
        return 0

    lax.fori_loop(0, 9, flip_w, 0)
    p32[:, pl.ds(0, FW), :] = jnp.zeros((2, FW, 128), F32)
    p32[:, pl.ds((H + 1) * FW, FW), :] = jnp.zeros((2, FW, 128), F32)
    for tw in range(8):
        q32[pl.ds(tw * QP, 8), :] = jnp.zeros((8, C), F32)
        q32[pl.ds(tw * QP + 8 + H, 8), :] = jnp.zeros((8, C), F32)
    pre[...] = jnp.zeros((2, 2 * HALF, 128), F32)

    def all_blocks(src, dst, sems):
        most = pl.ds(0, (n - 1) * FW)
        return to_tm(src.at[most], dst.at[most], sems, after)

    done_hid = all_blocks(hid, hidr, hid_sem)
    done_hid.wait_recv()
    theirs = pl.ds(pl.multiple_of((1 - core) * 128, 128), 128)
    mine = pl.ds(pl.multiple_of(core * 128, 128), 128)
    JQ = J // 4

    def quarter(q):
        return pl.ds(pl.multiple_of(q * C, C), C)

    def rows_of(j):
        return pl.ds(pl.multiple_of(j * CB, CB), CB)

    def swap(q):
        return to_tm(r1s.at[quarter(q)], r1r.at[quarter(q)], r1_sem.at[q], me + 1 - 2 * core)

    def send_pair(i, _):
        part = pl.ds(pl.multiple_of(i * 64, 64), 64)
        to_tm(r1s.at[part], r1r.at[part], r1_sem.at[i // 4], me + 1 - 2 * core).start()
        return 0

    def spread(q, _):
        swap(q).wait()
        total = keep[quarter(q), :] + r1r[quarter(q), :].astype(F32)
        keep[quarter(q), :] = total
        r2s[quarter(q), :] = total.astype(BF16)
        for i in range(JQ):
            j = q * JQ + i

            @pl.when(j != myj)
            def _():
                to_xy(r2s.at[rows_of(j)], r2r.at[rows_of(myj)], r2_sem, j).start()
        return 0

    r1s[...] = dot_nn(gt[...], hidr[:, theirs]).astype(BF16)
    lax.fori_loop(0, 16, send_pair, 0)
    keep[...] = dot_nn(gt[...], hidr[:, mine])
    lax.fori_loop(0, 4, spread, 0)

    most_xy = pl.ds(0, (J - 1) * CB)
    done_r2 = to_xy(r2s.at[most_xy], r2r.at[most_xy], r2_sem, lax.rem(myj + 1, J))
    done_r2.wait_recv()
    r2r[rows_of(myj), :] = jnp.zeros((CB, 128), BF16)
    total = keep[rows_of(myj), :]
    for j in range(J):
        total = total + r2r[pl.ds(j * CB, CB), :].astype(F32)
    flipped = jnp.concatenate([total.T, jnp.zeros((128, WIDE - CB), F32)], axis=1) if WIDE > CB else total.T
    for m in range(n // 2):
        r3s[m] = flipped[m * RB : (m + 1) * RB, :]

    z = me // 2

    def r3_copy(m):
        return pltpu.make_async_remote_copy(
            src_ref=r3s.at[m], dst_ref=r3r.at[z], send_sem=r3_send.at[m], recv_sem=r3_recv.at[z],
            device_id=(core * (n // 2) + m, dp, rep), device_id_type=MESH)

    def send_r3(m, _):
        @pl.when(core * (n // 2) + m != me)
        def _():
            r3_copy(m).start()

        @pl.when(core * (n // 2) + m == me)
        def _():
            r3r[z] = r3s[m]
        return 0

    lax.fori_loop(0, n // 2, send_r3, 0)

    done_hg = all_blocks(rg, hg, hg_sem)
    done_hg.wait_recv()

    def pre_grad(i, _):
        rows = pl.ds(pl.multiple_of(i * 64, 64), 64)
        grad = (hg[rows, :].astype(F32) * slope[rows, :]).astype(BF16).astype(F32)
        for e in range(2):
            p32[e, pl.ds(pl.multiple_of(FW + i * 64, FW), 64), :] = grad[:, LANES[e]]
        return 0

    lax.fori_loop(0, n // 4, pre_grad, 0)

    def grad_shifts(t, _):
        for col in range(4):
            for b in range(3):
                for e in range(2):
                    v = p32[e, pl.ds(b * FW + t * 4 + col, H, stride=FW), :].astype(BF16)
                    s[t, (col + 1) * H : (col + 2) * H, b * C + e * 128 : b * C + (e + 1) * 128] = v
        return 0

    lax.fori_loop(0, 2, grad_shifts, 0)
    for t in range(2):
        ph[pl.ds(t * 4 * H, 4 * H), :] = s[t, H : 5 * H, C : 2 * C]

    @pl.when(jnp.logical_not(is_first))
    def _():
        pieces(ph, phr, ph_sem, before)

    lax.fori_loop(2, 4, grad_shifts, 0)

    @pl.when(is_first)
    def _():
        two = s[0].astype(F32) + s[1].astype(F32)
        s[6] = two.astype(BF16)
        s[7] = (two + s[2].astype(F32)).astype(BF16)

    def conv_back(pair, a):
        first = a + 2 * pair
        edge = jnp.logical_and(is_first, jnp.logical_and(pair == 0, a > 0))
        taps(jnp.where(edge, a + 5, first), first + 1, pair, lambda c: wt[a * 3 + c])

    back = to_tm(ph, phr, ph_sem, before)

    def back_step(k, _):
        @pl.when(k == 4)
        def _():
            @pl.when(jnp.logical_not(is_last))
            def _():
                back.wait_recv()
                for tw in range(8):
                    q32[pl.ds(tw * QP + 8, H), :] = phr[pl.ds(tw * H, H), :].astype(F32)

            @pl.when(is_last)
            def _():
                for tw in range(8):
                    q32[pl.ds(tw * QP + 8, H), :] = jnp.zeros((H, C), F32)

            for t in range(2):
                for col in range(4):
                    for b in range(3):
                        v = q32[pl.ds((t * 4 + col) * QP + 7 + b, H), :].astype(BF16)
                        s[4 + t, (col + 1) * H : (col + 2) * H, b * C : (b + 1) * C] = v

        conv_back(jnp.where(k < 3, 0, 1), jnp.where(k < 3, k, k - 3))
        return 0

    lax.fori_loop(0, 6, back_step, 0)

    for t in range(4):
        for col in range(4):
            for e in range(2):
                of32[e, pl.ds(t * 4 * H + col, H, stride=4), :] = pre[e, pl.ds((t * 4 + col) * H, H), :]
    for e in range(2):
        out_ref[:, LANES[e]] = of32[e].astype(BF16)

    def wait_r3(i, _):
        @pl.when(2 * i + me // (n // 2) != me)
        def _():
            pltpu.make_async_remote_copy(
                src_ref=r3s.at[i], dst_ref=r3r.at[i], send_sem=r3_send.at[i], recv_sem=r3_recv.at[i],
                device_id=(after, dp, rep), device_id_type=MESH).wait_recv()

        @pl.when(core * (n // 2) + i != me)
        def _():
            r3_copy(i).wait_send()
        return 0

    lax.fori_loop(0, n // 2, wait_r3, 0)
    result = r3r[0]
    for i in range(1, n // 2):
        result = result + r3r[i]
    ug_ref[...] = result[:, 0:CB] * factor

    done_hid.wait_send()
    done_hg.wait_send()
    done_r2.wait_send()

    @pl.when(jnp.logical_not(is_last))
    def _():
        to_tm(hs, hf, hf_sem, after).wait_send()

    @pl.when(jnp.logical_not(is_first))
    def _():
        back.wait_send()


def local(n, J, R, clip_frames, conv_weight, up_weight, cotangent):
    C = conv_weight.shape[-1]
    H = n
    pixels = 16 * H
    factor = 1.0 / math.sqrt(J * 4 * n * H * 4)
    x = clip_frames.reshape(4 * H, 4, C)
    g = cotangent.reshape(4 * n, 4, 4 * C)
    vmem = pl.BlockSpec(memory_space=pltpu.VMEM)
    hbm = pl.BlockSpec(memory_space=pl.ANY)
    pair = pltpu.SemaphoreType.DMA((2,))
    out, up = pl.pallas_call(
        functools.partial(kernel, n, J, R, factor),
        out_shape=(
            jax.ShapeDtypeStruct((pixels, C), BF16),
            jax.ShapeDtypeStruct((C // n, 4 * C // J), F32),
        ),
        in_specs=[hbm, hbm, hbm, hbm],
        out_specs=(vmem, vmem),
        scratch_shapes=[
            pltpu.VMEM((4 * H, 4, C), BF16),
            pltpu.VMEM((4 * n, 4, 4 * C), BF16),
            pltpu.VMEM((16 * n, 4 * C), BF16),
            pltpu.VMEM((C, 4 * C), BF16),
            pltpu.VMEM((3, 3, 3, C, C), BF16),
            pltpu.VMEM((9, 3 * C, C), BF16),
            pltpu.VMEM((4 * C, 16 * n), BF16),
            pltpu.VMEM((16 * n, C), BF16),
            pltpu.VMEM((16 * n, C), BF16),
            pltpu.VMEM((16 * n, C), BF16),
            pltpu.VMEM((16 * n, C), BF16),
            pltpu.VMEM((8 * H, C), BF16),
            pltpu.VMEM((8 * H, C), BF16),
            pltpu.VMEM((8 * H, C), BF16),
            pltpu.VMEM((8 * H, C), BF16),
            pltpu.VMEM((2, 6 * (4 * H + 16), 128), F32),
            pltpu.VMEM((2, (H + 2) * 16, 128), F32),
            pltpu.VMEM((8 * (H + 16), C), F32),
            pltpu.VMEM((8, 6 * H, 3 * C), BF16),
            pltpu.VMEM((2, pixels, 128), F32),
            pltpu.VMEM((pixels, C), F32),
            pltpu.VMEM((2, pixels, 128), F32),
            pltpu.VMEM((4 * C, C // 2), BF16),
            pltpu.VMEM((4 * C, C // 2), BF16),
            pltpu.VMEM((4 * C, C // 2), F32),
            pltpu.VMEM((4 * C, C // 2), BF16),
            pltpu.VMEM((4 * C, C // 2), BF16),
            pltpu.VMEM((n // 2, C // n, max(128, 4 * C // J)), F32),
            pltpu.VMEM((n // 2, C // n, max(128, 4 * C // J)), F32),
            pltpu.SemaphoreType.DMA((15,)),
            pair, pair, pair, pair,
            pltpu.SemaphoreType.DMA((4, 2)),
            pair,
            pltpu.SemaphoreType.DMA((n // 2,)),
            pltpu.SemaphoreType.DMA((n // 2,)),
        ],
        compiler_params=pltpu.CompilerParams(
            collective_id=0, has_side_effects=True, vmem_limit_bytes=56098816),
        cost_estimate=pl.CostEstimate(flops=4_200_000_000, bytes_accessed=6_000_000, transcendentals=131072),
    )(x, conv_weight, up_weight, g)
    return out.reshape(clip_frames.shape), up


def solution(mesh):
    in_specs = (
        P(("dp", "rep"), "tm", None, None, None),
        P(),
        P(),
        P(("dp", "rep"), None, "tm", None, None),
    )
    out_specs = (P(("dp", "rep"), "tm", None, None, None), P("tm", ("dp", "rep")))
    n = mesh.shape["tm"]
    R = mesh.shape["rep"]
    J = mesh.shape["dp"] * R
    return jax.shard_map(functools.partial(local, n, J, R), mesh=mesh, in_specs=in_specs,
                         out_specs=out_specs, check_vma=False)
```

time: 72.7 us -> 55.2 us (0.76)
  Pallas kernels: 65 us -> 53.1 us
  local copies, waits for them, and re-layouts: 6.76 us -> 1.36 us
    pallas_call x1, Pallas kernels: 65 us -> 53.1 us  [local(): pl.pallas_call(functools.partial(kernel, n, J, R, factor), out_shape=(jax...]
    unnamed x5 -> x1, local copies, waits for them, and re-layouts: 3.63 us -> 0.59 us
    reshape x2 -> x0, local copies, waits for them, and re-layouts: 2.36 us -> none  [the longest x1 1.34 us: local(): g = cotangent.reshape(16 * n, 4 * C)]
where the time goes in v2:
time: 55.2 us; the launch traced here: 55.1 us
  Pallas kernels  53.1 us (96%)
  local copies, waits for them, and re-layouts  1.36 us (2%)
  between operations  0.64 us (1%)
    pallas_call x1, Pallas kernels, local(): pl.pallas_call(functools.partial(kernel, n, J, R, factor), out_shape=(jax...  53.1 us

profile of v2, /device:TPU:1, one launch (start us, length us, event | category | flops | bytes accessed | tf_op | source)
XLA Modules:
  0.0 55.1 jit_solution(6476989791310474078)
XLA Ops:
  0.6 53.1 %shard_map.59 = (bf16[512,256]{1,0:T(8,128)(2,1)S(1)}, f32[8,64]{1,0:T(8,128)S(1)}) custom-call(bf16[128,4,256]{2,1,0:T(4,128)(2,1)} %bitcast.3, bf16[3,3,3,256,256]{4,3,2,1,0:T(8,128)(2,1)} %w_hbm.1, bf16[256,1024]{1,0:T(8,128)(2,1)} %u_hbm.1, bf16[128,4,1024]{2,1,0:T(4,128)(2,1)} %bitcast.2), custom_call_target="tpu_custom_call" | custom-call | flops 4200000000 | bytes 6000000 | tf_op jit(solution)/shard_map/pallas_call | solution.py:419
  53.7 0.8 %reshape.15 = bf16[1,4,32,4,256]{4,3,2,1,0:T(4,128)(2,1)} reshape(bf16[512,256]{1,0:T(8,128)(2,1)S(1)} %get-tuple-element.4) | data formatting | bytes 524288 | tf_op jit(solution)/shard_map/reshape | solution.py:468
  54.5 0.6 %copy.7 = f32[8,64]{1,0:T(8,128)} copy(f32[8,64]{1,0:T(8,128)S(1)} %get-tuple-element.9) | data formatting | bytes 4096

commit v3 on v2

--- a/solution.py
+++ b/solution.py
@@ -12,6 +12,7 @@
 BF16 = jnp.bfloat16
 F32 = jnp.float32
 LANES = (slice(0, 128), slice(128, 256))
+SOON = 10
 
 
 def dot_nn(a, b):
@@ -33,8 +34,9 @@
     XP = 4 * H + 16
     QP = H + 16
     CB = 4 * C // J
-    WIDE = -(-CB // 128) * 128
     RB = C // n
+    FOLD = max(1, 128 // CB)
+    RF = RB // FOLD
     me = lax.axis_index("tm")
     dp = lax.axis_index("dp")
     rep = lax.axis_index("rep")
@@ -204,7 +206,8 @@
         to_tm(rg.at[block(to)], hg.at[block(me)], hg_sem, to).start()
         return 0
 
-    lax.fori_loop(1, n, send_hg, 0)
+    soon = min(SOON + 1, n)
+    lax.fori_loop(1, soon, send_hg, 0)
     hidr[block(me), :] = hid[block(me), :]
 
     def flip_g(i, _):
@@ -234,6 +237,7 @@
 
     done_hid = all_blocks(hid, hidr, hid_sem)
     done_hid.wait_recv()
+    lax.fori_loop(soon, n, send_hg, 0)
     theirs = pl.ds(pl.multiple_of((1 - core) * 128, 128), 128)
     mine = pl.ds(pl.multiple_of(core * 128, 128), 128)
     JQ = J // 4
@@ -277,9 +281,10 @@
     total = keep[rows_of(myj), :]
     for j in range(J):
         total = total + r2r[pl.ds(j * CB, CB), :].astype(F32)
-    flipped = jnp.concatenate([total.T, jnp.zeros((128, WIDE - CB), F32)], axis=1) if WIDE > CB else total.T
+    flipped = total.T
     for m in range(n // 2):
-        r3s[m] = flipped[m * RB : (m + 1) * RB, :]
+        for i in range(FOLD):
+            r3s[m, :, i * CB : (i + 1) * CB] = flipped[m * RB + i * RF : m * RB + (i + 1) * RF, :]
 
     z = me // 2
 
@@ -391,7 +396,8 @@
     result = r3r[0]
     for i in range(1, n // 2):
         result = result + r3r[i]
-    ug_ref[...] = result[:, 0:CB] * factor
+    for i in range(FOLD):
+        ug_ref[i * RF : (i + 1) * RF, :] = result[:, i * CB : (i + 1) * CB] * factor
 
     done_hid.wait_send()
     done_hg.wait_send()
@@ -410,6 +416,7 @@
     C = conv_weight.shape[-1]
     H = n
     pixels = 16 * H
+    fold = max(1, 128 * J // (4 * C))
     factor = 1.0 / math.sqrt(J * 4 * n * H * 4)
     x = clip_frames.reshape(4 * H, 4, C)
     g = cotangent.reshape(4 * n, 4, 4 * C)
@@ -452,8 +459,8 @@
             pltpu.VMEM((4 * C, C // 2), F32),
             pltpu.VMEM((4 * C, C // 2), BF16),
             pltpu.VMEM((4 * C, C // 2), BF16),
-            pltpu.VMEM((n // 2, C // n, max(128, 4 * C // J)), F32),
-            pltpu.VMEM((n // 2, C // n, max(128, 4 * C // J)), F32),
+            pltpu.VMEM((n // 2, C // n // fold, fold * 4 * C // J), F32),
+            pltpu.VMEM((n // 2, C // n // fold, fold * 4 * C // J), F32),
             pltpu.SemaphoreType.DMA((15,)),
             pair, pair, pair, pair,
             pltpu.SemaphoreType.DMA((4, 2)),

time: 55.2 us -> 54 us (0.978)
  Pallas kernels: 53.1 us -> 51.9 us
    pallas_call x1, Pallas kernels: 53.1 us -> 51.9 us  [local(): pl.pallas_call(functools.partial(kernel, n, J, R, factor), out_shape=(jax...]
where the time goes in v3:
time: 54 us; the launch traced here: 53.9 us
  Pallas kernels  51.9 us (96%)
  local copies, waits for them, and re-layouts  1.36 us (3%)
  between operations  0.64 us (1%)
    pallas_call x1, Pallas kernels, local(): pl.pallas_call(functools.partial(kernel, n, J, R, factor), out_shape=(jax...  51.9 us

profile of v3, /device:TPU:1, one launch (start us, length us, event | category | flops | bytes accessed | tf_op | source)
XLA Modules:
  0.0 53.9 jit_solution(14299677957819240322)
XLA Ops:
  0.6 51.9 %shard_map.59 = (bf16[512,256]{1,0:T(8,128)(2,1)S(1)}, f32[8,64]{1,0:T(8,128)S(1)}) custom-call(bf16[128,4,256]{2,1,0:T(4,128)(2,1)} %bitcast.3, bf16[3,3,3,256,256]{4,3,2,1,0:T(8,128)(2,1)} %w_hbm.1, bf16[256,1024]{1,0:T(8,128)(2,1)} %u_hbm.1, bf16[128,4,1024]{2,1,0:T(4,128)(2,1)} %bitcast.2), custom_call_target="tpu_custom_call" | custom-call | flops 4200000000 | bytes 6000000 | tf_op jit(solution)/shard_map/pallas_call | solution.py:426
  52.5 0.8 %reshape.15 = bf16[1,4,32,4,256]{4,3,2,1,0:T(4,128)(2,1)} reshape(bf16[512,256]{1,0:T(8,128)(2,1)S(1)} %get-tuple-element.4) | data formatting | bytes 524288 | tf_op jit(solution)/shard_map/reshape | solution.py:475
  53.3 0.6 %copy.7 = f32[8,64]{1,0:T(8,128)} copy(f32[8,64]{1,0:T(8,128)S(1)} %get-tuple-element.9) | data formatting | bytes 4096

commit v4 on v3

--- a/solution.py
+++ b/solution.py
@@ -177,7 +177,6 @@
                 v = pre[e, pl.ds(to, FW, stride=H), :]
                 sig = 0.5 + 0.5 * jnp.tanh(0.5 * v)
                 hid[block(to), LANES[e]] = (v * sig).astype(BF16)
-                slope[block(to), LANES[e]] = sig * (1.0 + v * (1.0 - sig))
         for i in range(4):
             k = group * 4 + i + 1
             to = peer(k)
@@ -224,6 +223,17 @@
         return 0
 
     lax.fori_loop(0, 9, flip_w, 0)
+
+    def slopes(group, _):
+        for i in range(4):
+            row = group * 4 + i
+            for e in range(2):
+                v = pre[e, pl.ds(row, FW, stride=H), :]
+                sig = 0.5 + 0.5 * jnp.tanh(0.5 * v)
+                slope[block(row), LANES[e]] = sig * (1.0 + v * (1.0 - sig))
+        return 0
+
+    lax.fori_loop(0, n // 4, slopes, 0)
     p32[:, pl.ds(0, FW), :] = jnp.zeros((2, FW, 128), F32)
     p32[:, pl.ds((H + 1) * FW, FW), :] = jnp.zeros((2, FW, 128), F32)
     for tw in range(8):
@@ -237,7 +247,6 @@
 
     done_hid = all_blocks(hid, hidr, hid_sem)
     done_hid.wait_recv()
-    lax.fori_loop(soon, n, send_hg, 0)
     theirs = pl.ds(pl.multiple_of((1 - core) * 128, 128), 128)
     mine = pl.ds(pl.multiple_of(core * 128, 128), 128)
     JQ = J // 4
@@ -271,6 +280,7 @@
 
     r1s[...] = dot_nn(gt[...], hidr[:, theirs]).astype(BF16)
     lax.fori_loop(0, 16, send_pair, 0)
+    lax.fori_loop(soon, n, send_hg, 0)
     keep[...] = dot_nn(gt[...], hidr[:, mine])
     lax.fori_loop(0, 4, spread, 0)
 

time: 54 us -> 53.7 us (level)
  no operation moved by 1% of the time
where the time goes in v4:
time: 53.7 us; the launch traced here: 53.5 us
  Pallas kernels  51.5 us (96%)
  local copies, waits for them, and re-layouts  1.36 us (3%)
  between operations  0.64 us (1%)
    pallas_call x1, Pallas kernels, local(): pl.pallas_call(functools.partial(kernel, n, J, R, factor), out_shape=(jax...  51.5 us

profile of v4, /device:TPU:1, one launch (start us, length us, event | category | flops | bytes accessed | tf_op | source)
XLA Modules:
  0.0 53.5 jit_solution(7112672990366328866)
XLA Ops:
  0.6 51.5 %shard_map.59 = (bf16[512,256]{1,0:T(8,128)(2,1)S(1)}, f32[8,64]{1,0:T(8,128)S(1)}) custom-call(bf16[128,4,256]{2,1,0:T(4,128)(2,1)} %bitcast.3, bf16[3,3,3,256,256]{4,3,2,1,0:T(8,128)(2,1)} %w_hbm.1, bf16[256,1024]{1,0:T(8,128)(2,1)} %u_hbm.1, bf16[128,4,1024]{2,1,0:T(4,128)(2,1)} %bitcast.2), custom_call_target="tpu_custom_call" | custom-call | flops 4200000000 | bytes 6000000 | tf_op jit(solution)/shard_map/pallas_call | solution.py:436
  52.2 0.8 %reshape.15 = bf16[1,4,32,4,256]{4,3,2,1,0:T(4,128)(2,1)} reshape(bf16[512,256]{1,0:T(8,128)(2,1)S(1)} %get-tuple-element.4) | data formatting | bytes 524288 | tf_op jit(solution)/shard_map/reshape | solution.py:485
  52.9 0.6 %copy.7 = f32[8,64]{1,0:T(8,128)} copy(f32[8,64]{1,0:T(8,128)S(1)} %get-tuple-element.9) | data formatting | bytes 4096
